TPU v7x, 32 devices: a whole 2x2x4 slice. The times are simulated.
32 devices in a mesh: leaf: 16 (over z, y, x), rhs: 2 (over core).
Axes of the slice: x: 2, y: 2, z: 4, core: 2. Of those that a mesh axis runs over, the one named last changes fastest.
Arguments:
- leaf_skel: bfloat16 [2, 16, 128, 512], P(None, 'leaf', 'rhs'), may hold values from -6 to 6
- ranks: int32 [2, 16, 5], P(None, 'leaf'), may hold values from 64 to 256, as said below
- up_weight: bfloat16 [2, 15360, 512], P(None, 'leaf', 'rhs'), may hold values from -0.1875 to 0.1875
- down_weight: bfloat16 [2, 31232, 512], P(None, 'leaf', 'rhs'), may hold values from -1 to 1
Outputs:
- leaf_result: bfloat16 [2, 16, 128, 512], P(None, 'leaf', 'rhs')
Inputs may be any that keep to these rules, and one draw needn't show every extreme that they name: ranks[b, i, l] is the rank of the level-l node above leaf i of tree b: equal for all leaves under one node; some node reaches 256.
All inputs are finite; a program needn't handle non-finite values.
Results may differ from a plain program's by a relative error of at most 0.022.
Values may be sent and summed in bfloat16 or wider, within the bound.
A program may use at most 64 MiB of HBM per device.

v0:
```python
import jax
import jax.numpy as jnp
from jax import lax
from jax.sharding import PartitionSpec as P


def partner(block, axis, distance):
    count = lax.axis_size(axis)
    route = []
    for low in range(count):
        high = low | 1 << distance
        if high != low and high < count:
            route += [(low, high), (high, low)]
    return lax.ppermute(block, axis, route)


def keep_columns(rank_col, width):
    column_ids = jnp.arange(width) % (width // 2)
    return column_ids[None, None, :] < rank_col[:, None, None]


def project_with(block, piece):
    return jnp.einsum("bcr,brm->bcm", block, piece, preferred_element_type=jnp.float32)


def settle_up(total, nbits, keep):
    for level_bit in range(nbits):
        total = total + partner(total.astype(jnp.bfloat16), "leaf", level_bit).astype(total.dtype)
    return jnp.where(keep, total, 0.0).astype(jnp.bfloat16)


def settle_down(total, nbits, keep):
    for level_bit in range(nbits):
        total = total + partner(total.astype(jnp.bfloat16), "leaf", level_bit).astype(total.dtype)
    return jnp.where(keep, total, 0.0).astype(jnp.bfloat16)


def per_device(leaf_skel, ranks, up_weight, down_weight):
    position = lax.axis_index("leaf")
    width_all = leaf_skel.shape[-1]
    levels = ranks.shape[-1] - 1
    node_ranks = ranks[:, 0, :]
    current = jnp.where(keep_columns(node_ranks[:, 0], width_all), leaf_skel[:, 0], 0.0)
    saved = [current]
    for level in range(levels):
        width = width_all >> level
        offset = 2 * width_all - (2 * width_all >> level)
        member = position % (1 << level)
        block = lax.dynamic_slice_in_dim(current, member * width, width, 2)
        factor_rows = up_weight[:, offset : offset + width, :]
        partial_value = project_with(block, lax.all_gather(factor_rows, "rhs", axis=2, tiled=True))
        current = settle_up(
            partial_value, level + 1, keep_columns(node_ranks[:, level + 1], width_all)
        )
        saved.append(current)
    width = width_all >> levels
    member = position % (1 << levels)
    block = lax.dynamic_slice_in_dim(saved[levels], member * width, width, 2)
    factor_rows = down_weight[:, :width, :]
    partial_value = project_with(block, lax.all_gather(factor_rows, "rhs", axis=2, tiled=True))
    result = settle_down(partial_value, levels, keep_columns(node_ranks[:, levels], width_all))
    for level in reversed(range(levels)):
        width = width_all >> level
        offset = (width_all >> levels) + 2 * (2 * width_all - (2 * width_all >> level))
        member = position % (1 << level)
        own_part = lax.dynamic_slice_in_dim(saved[level], member * width, width, 2)
        parent_part = lax.dynamic_slice_in_dim(result, member * width, width, 2)
        block = jnp.concatenate([own_part, parent_part], 2)
        factor_rows = down_weight[:, offset : offset + 2 * width, :]
        partial_value = project_with(block, lax.all_gather(factor_rows, "rhs", axis=2, tiled=True))
        result = settle_down(partial_value, level, keep_columns(node_ranks[:, level], width_all))
    return result[:, None]


def solution(mesh):
    return jax.shard_map(
        per_device,
        mesh=mesh,
        in_specs=(
            P(None, "leaf", "rhs", None),
            P(None, "leaf", None),
            P(None, "leaf", "rhs"),
            P(None, "leaf", "rhs"),
        ),
        out_specs=P(None, "leaf", "rhs", None),
        check_vma=False,
    )
```

profile of v0, /device:TPU:0, one launch (start us, length us, event | category | flops | bytes accessed | tf_op | source)
XLA Modules:
  0.0 142.1 jit_solution(17982315517107232809)
XLA Ops:
  9.0 11.6 %all-gather.4.cloned.1.call-done = bf16[2,512,512]{2,1,0:T(8,128)(2,1)} async-done(((bf16[2,512,256]{2,1,0:T(8,128)(2,1)}), bf16[2,512,512]{2,1,0:T(8,128)(2,1)}) %all-gather.4.cloned.1.call-update) | async-done | bytes 1048592 | tf_op jit(solution)/shard_map/all_gather | solution.py:51
  24.0 2.2 %all_gather.28 = bf16[2,256,512]{2,1,0:T(8,128)(2,1)S(1)} all-gather(bf16[2,256,256]{2,1,0:T(8,128)(2,1)S(1)} %slice-done.3), channel_id=1, replica_groups=mesh['leaf'=16,'rhs'=2] {'rhs'}, dimensions={2}, use_global_device_ids=true | all-gather | bytes 786432 | tf_op jit(solution)/shard_map/all_gather | solution.py:51
  30.0 3.2 %collective-permute-done.1 = bf16[2,64,512]{2,1,0:T(8,128)(2,1)S(1)} collective-permute-done((bf16[2,64,512]{2,1,0:T(8,128)(2,1)S(1)}, bf16[2,64,512]{2,1,0:T(8,128)(2,1)S(1)}, u32[]{:S(2)}, u32[]{:S(2)}) %collective-permute-start.1) | collective-permute-done | bytes 131104 | tf_op jit(solution)/shard_map/ppermute | solution.py:14
  35.0 2.0 %all_gather.29 = bf16[2,128,512]{2,1,0:T(8,128)(2,1)S(1)} all-gather(bf16[2,128,256]{2,1,0:T(8,128)(2,1)S(1)} %slice-done.4), channel_id=1, replica_groups=mesh['leaf'=16,'rhs'=2] {'rhs'}, dimensions={2}, use_global_device_ids=true | all-gather | bytes 393216 | tf_op jit(solution)/shard_map/all_gather | solution.py:51
  40.3 3.2 %collective-permute-done.3 = bf16[2,64,512]{2,1,0:T(8,128)(2,1)S(1)} collective-permute-done((bf16[2,64,512]{2,1,0:T(8,128)(2,1)S(1)}, bf16[2,64,512]{2,1,0:T(8,128)(2,1)S(1)}, u32[]{:S(2)}, u32[]{:S(2)}) %collective-permute-start.3) | collective-permute-done | bytes 131104 | tf_op jit(solution)/shard_map/ppermute | solution.py:14
  45.3 3.2 %collective-permute-done.4 = bf16[2,64,512]{2,1,0:T(8,128)(2,1)S(1)} collective-permute-done((bf16[2,64,512]{2,1,0:T(8,128)(2,1)S(1)}, bf16[2,64,512]{2,1,0:T(8,128)(2,1)S(1)}, u32[]{:S(2)}, u32[]{:S(2)}) %collective-permute-start.4) | collective-permute-done | bytes 131104 | tf_op jit(solution)/shard_map/ppermute | solution.py:14
  55.7 3.2 %collective-permute-done.6 = bf16[2,64,512]{2,1,0:T(8,128)(2,1)S(1)} collective-permute-done((bf16[2,64,512]{2,1,0:T(8,128)(2,1)S(1)}, bf16[2,64,512]{2,1,0:T(8,128)(2,1)S(1)}, u32[]{:S(2)}, u32[]{:S(2)}) %collective-permute-start.6) | collective-permute-done | bytes 131104 | tf_op jit(solution)/shard_map/ppermute | solution.py:14
  60.8 3.2 %collective-permute-done.7 = bf16[2,64,512]{2,1,0:T(8,128)(2,1)S(1)} collective-permute-done((bf16[2,64,512]{2,1,0:T(8,128)(2,1)S(1)}, bf16[2,64,512]{2,1,0:T(8,128)(2,1)S(1)}, u32[]{:S(2)}, u32[]{:S(2)}) %collective-permute-start.7) | collective-permute-done | bytes 131104 | tf_op jit(solution)/shard_map/ppermute | solution.py:14
  65.9 3.6 %collective-permute-done.8 = bf16[2,64,512]{2,1,0:T(8,128)(2,1)S(1)} collective-permute-done((bf16[2,64,512]{2,1,0:T(8,128)(2,1)S(1)}, bf16[2,64,512]{2,1,0:T(8,128)(2,1)S(1)}, u32[]{:S(2)}, u32[]{:S(2)}) %collective-permute-start.8) | collective-permute-done | bytes 131104 | tf_op jit(solution)/shard_map/ppermute | solution.py:14
  69.6 2.3 %collective-permute-start.9 = (bf16[2,64,512]{2,1,0:T(8,128)(2,1)S(1)}, bf16[2,64,512]{2,1,0:T(8,128)(2,1)S(1)}, u32[]{:S(2)}, u32[]{:S(2)}) collective-permute-start(bf16[2,64,512]{2,1,0:T(8,128)(2,1)S(1)} %get-tuple-element.16), channel_id=1, source_target_pairs={{0,16},{16,0},{2,18},{18,2},{4,20},{20,4},{6,22},{22,6},{8,24},{24... | collective-permute-start | bytes 393224 | tf_op jit(solution)/shard_map/ppermute | solution.py:14
  77.6 3.3 %collective-permute-done.10 = bf16[2,64,512]{2,1,0:T(8,128)(2,1)S(1)} collective-permute-done((bf16[2,64,512]{2,1,0:T(8,128)(2,1)S(1)}, bf16[2,64,512]{2,1,0:T(8,128)(2,1)S(1)}, u32[]{:S(2)}, u32[]{:S(2)}) %collective-permute-start.10) | collective-permute-done | bytes 131104 | tf_op jit(solution)/shard_map/ppermute | solution.py:14
  82.6 3.3 %collective-permute-done.11 = bf16[2,64,512]{2,1,0:T(8,128)(2,1)S(1)} collective-permute-done((bf16[2,64,512]{2,1,0:T(8,128)(2,1)S(1)}, bf16[2,64,512]{2,1,0:T(8,128)(2,1)S(1)}, u32[]{:S(2)}, u32[]{:S(2)}) %collective-permute-start.11) | collective-permute-done | bytes 131104 | tf_op jit(solution)/shard_map/ppermute | solution.py:14
  86.0 2.5 %collective-permute-start.12 = (bf16[2,64,512]{2,1,0:T(8,128)(2,1)S(1)}, bf16[2,64,512]{2,1,0:T(8,128)(2,1)S(1)}, u32[]{:S(2)}, u32[]{:S(2)}) collective-permute-start(bf16[2,64,512]{2,1,0:T(8,128)(2,1)S(1)} %fusion.18), channel_id=1, source_target_pairs={{0,8},{8,0},{2,10},{10,2},{4,12},{12,4},{6,14},{14,6},{16,24},{24,... | collective-permute-start | bytes 393224 | tf_op jit(solution)/shard_map/ppermute | solution.py:14
  89.4 3.4 %collective-permute-done.12 = bf16[2,64,512]{2,1,0:T(8,128)(2,1)S(1)} collective-permute-done((bf16[2,64,512]{2,1,0:T(8,128)(2,1)S(1)}, bf16[2,64,512]{2,1,0:T(8,128)(2,1)S(1)}, u32[]{:S(2)}, u32[]{:S(2)}) %collective-permute-start.12) | collective-permute-done | bytes 131104 | tf_op jit(solution)/shard_map/ppermute | solution.py:14
  92.9 2.1 %collective-permute-start.13 = (bf16[2,64,512]{2,1,0:T(8,128)(2,1)S(1)}, bf16[2,64,512]{2,1,0:T(8,128)(2,1)S(1)}, u32[]{:S(2)}, u32[]{:S(2)}) collective-permute-start(bf16[2,64,512]{2,1,0:T(8,128)(2,1)S(1)} %get-tuple-element.14), channel_id=1, source_target_pairs={{0,16},{16,0},{2,18},{18,2},{4,20},{20,4},{6,22},{22,6},{8,24},{24... | collective-permute-start | bytes 393224 | tf_op jit(solution)/shard_map/ppermute | solution.py:14
  97.1 3.1 %collective-permute-done.13 = bf16[2,64,512]{2,1,0:T(8,128)(2,1)S(1)} collective-permute-done((bf16[2,64,512]{2,1,0:T(8,128)(2,1)S(1)}, bf16[2,64,512]{2,1,0:T(8,128)(2,1)S(1)}, u32[]{:S(2)}, u32[]{:S(2)}) %collective-permute-start.13) | collective-permute-done | bytes 131104 | tf_op jit(solution)/shard_map/ppermute | solution.py:14
  102.1 3.5 %collective-permute-done.14 = bf16[2,64,512]{2,1,0:T(8,128)(2,1)S(1)} collective-permute-done((bf16[2,64,512]{2,1,0:T(8,128)(2,1)S(1)}, bf16[2,64,512]{2,1,0:T(8,128)(2,1)S(1)}, u32[]{:S(2)}, u32[]{:S(2)}) %collective-permute-start.14) | collective-permute-done | bytes 131104 | tf_op jit(solution)/shard_map/ppermute | solution.py:14
  108.3 2.4 %collective-permute-done.15 = bf16[2,64,512]{2,1,0:T(8,128)(2,1)S(1)} collective-permute-done((bf16[2,64,512]{2,1,0:T(8,128)(2,1)S(1)}, bf16[2,64,512]{2,1,0:T(8,128)(2,1)S(1)}, u32[]{:S(2)}, u32[]{:S(2)}) %collective-permute-start.15) | collective-permute-done | bytes 131104 | tf_op jit(solution)/shard_map/ppermute | solution.py:14
  111.1 2.2 %all_gather.33 = bf16[2,256,512]{2,1,0:T(8,128)(2,1)S(1)} all-gather(bf16[2,256,256]{2,1,0:T(8,128)(2,1)S(1)} %slice-done.2), channel_id=1, replica_groups=mesh['leaf'=16,'rhs'=2] {'rhs'}, dimensions={2}, use_global_device_ids=true | all-gather | bytes 786432 | tf_op jit(solution)/shard_map/all_gather | solution.py:70
  113.2 2.5 %collective-permute-done.16 = bf16[2,64,512]{2,1,0:T(8,128)(2,1)S(1)} collective-permute-done((bf16[2,64,512]{2,1,0:T(8,128)(2,1)S(1)}, bf16[2,64,512]{2,1,0:T(8,128)(2,1)S(1)}, u32[]{:S(2)}, u32[]{:S(2)}) %collective-permute-start.16) | collective-permute-done | bytes 131104 | tf_op jit(solution)/shard_map/ppermute | solution.py:14
  117.6 3.5 %collective-permute-done.17 = bf16[2,64,512]{2,1,0:T(8,128)(2,1)S(1)} collective-permute-done((bf16[2,64,512]{2,1,0:T(8,128)(2,1)S(1)}, bf16[2,64,512]{2,1,0:T(8,128)(2,1)S(1)}, u32[]{:S(2)}, u32[]{:S(2)}) %collective-permute-start.17) | collective-permute-done | bytes 131104 | tf_op jit(solution)/shard_map/ppermute | solution.py:14
  122.6 3.5 %collective-permute-done.18 = bf16[2,64,512]{2,1,0:T(8,128)(2,1)S(1)} collective-permute-done((bf16[2,64,512]{2,1,0:T(8,128)(2,1)S(1)}, bf16[2,64,512]{2,1,0:T(8,128)(2,1)S(1)}, u32[]{:S(2)}, u32[]{:S(2)}) %collective-permute-start.18) | collective-permute-done | bytes 131104 | tf_op jit(solution)/shard_map/ppermute | solution.py:14
  129.3 3.5 %collective-permute-done.19 = bf16[2,64,512]{2,1,0:T(8,128)(2,1)S(1)} collective-permute-done((bf16[2,64,512]{2,1,0:T(8,128)(2,1)S(1)}, bf16[2,64,512]{2,1,0:T(8,128)(2,1)S(1)}, u32[]{:S(2)}, u32[]{:S(2)}) %collective-permute-start.19) | collective-permute-done | bytes 131104 | tf_op jit(solution)/shard_map/ppermute | solution.py:14
  132.8 2.7 %fusion.1 = bf16[2,1,64,512]{3,2,1,0:T(8,128)(2,1)} fusion(bf16[2,1024,512]{2,1,0:T(8,128)(2,1)} %all-gather.8.cloned.1.call-done, bf16[2,64,512]{2,1,0:T(8,128)(2,1)S(1)} %select_convert_fusion, bf16[2,64,512]{2,1,0:T(8,128)(2,1)S(1)} %bitcast_select_fusion, pred[2,512]{1,0:T(4,128)(4,1)S(1)} %get-tuple-element.26), kind=kOutput, calls=%fused_computation.2 | convolution fusion | flops 134873088 | bytes 2491392 | tf_op jit(solution)/shard_map/bcr,brm->bcm/dot_general | solution.py:23
  (91 shorter events, 49.2 us)
Async XLA Ops:
  6.5 14.1 %all-gather.4.cloned.1.call-start = ((), (), s32[]{:S(2)}) async-start(), calls=%async_computation | async-start | bytes 1572864 | tf_op jit(solution)/shard_map/all_gather | solution.py:51
  8.5 117.7 %all-gather.6.cloned.1.call-start = ((), (), s32[]{:S(2)}) async-start(), calls=%async_computation.1 | async-start | bytes 1572864 | tf_op jit(solution)/shard_map/all_gather | solution.py:70
  22.2 5.8 %collective-permute-start = (bf16[2,64,512]{2,1,0:T(8,128)(2,1)S(1)}, bf16[2,64,512]{2,1,0:T(8,128)(2,1)S(1)}, u32[]{:S(2)}, u32[]{:S(2)}) collective-permute-start(bf16[2,64,512]{2,1,0:T(8,128)(2,1)S(1)} %get-tuple-element.27), channel_id=1, source_target_pairs={{0,2},{2,0},{4,6},{6,4},{8,10},{10,8},{12,14},{14,12},{16,18},{18,... | collective-permute-start | bytes 393224 | tf_op jit(solution)/shard_map/ppermute | solution.py:14
  28.2 5.0 %collective-permute-start.1 = (bf16[2,64,512]{2,1,0:T(8,128)(2,1)S(1)}, bf16[2,64,512]{2,1,0:T(8,128)(2,1)S(1)}, u32[]{:S(2)}, u32[]{:S(2)}) collective-permute-start(bf16[2,64,512]{2,1,0:T(8,128)(2,1)S(1)} %get-tuple-element.29), channel_id=1, source_target_pairs={{0,2},{2,0},{4,6},{6,4},{8,10},{10,8},{12,14},{14,12},{16,18},{18,... | collective-permute-start | bytes 393224 | tf_op jit(solution)/shard_map/ppermute | solution.py:14
  33.2 5.0 %collective-permute-start.2 = (bf16[2,64,512]{2,1,0:T(8,128)(2,1)S(1)}, bf16[2,64,512]{2,1,0:T(8,128)(2,1)S(1)}, u32[]{:S(2)}, u32[]{:S(2)}) collective-permute-start(bf16[2,64,512]{2,1,0:T(8,128)(2,1)S(1)} %get-tuple-element.20), channel_id=1, source_target_pairs={{0,4},{4,0},{2,6},{6,2},{8,12},{12,8},{10,14},{14,10},{16,20},{20,... | collective-permute-start | bytes 393224 | tf_op jit(solution)/shard_map/ppermute | solution.py:14
  38.5 5.0 %collective-permute-start.3 = (bf16[2,64,512]{2,1,0:T(8,128)(2,1)S(1)}, bf16[2,64,512]{2,1,0:T(8,128)(2,1)S(1)}, u32[]{:S(2)}, u32[]{:S(2)}) collective-permute-start(bf16[2,64,512]{2,1,0:T(8,128)(2,1)S(1)} %get-tuple-element.31), channel_id=1, source_target_pairs={{0,2},{2,0},{4,6},{6,4},{8,10},{10,8},{12,14},{14,12},{16,18},{18,... | collective-permute-start | bytes 393224 | tf_op jit(solution)/shard_map/ppermute | solution.py:14
  43.5 5.0 %collective-permute-start.4 = (bf16[2,64,512]{2,1,0:T(8,128)(2,1)S(1)}, bf16[2,64,512]{2,1,0:T(8,128)(2,1)S(1)}, u32[]{:S(2)}, u32[]{:S(2)}) collective-permute-start(bf16[2,64,512]{2,1,0:T(8,128)(2,1)S(1)} %fusion.5), channel_id=1, source_target_pairs={{0,4},{4,0},{2,6},{6,2},{8,12},{12,8},{10,14},{14,10},{16,20},{20,... | collective-permute-start | bytes 393224 | tf_op jit(solution)/shard_map/ppermute | solution.py:14
  48.6 5.0 %collective-permute-start.5 = (bf16[2,64,512]{2,1,0:T(8,128)(2,1)S(1)}, bf16[2,64,512]{2,1,0:T(8,128)(2,1)S(1)}, u32[]{:S(2)}, u32[]{:S(2)}) collective-permute-start(bf16[2,64,512]{2,1,0:T(8,128)(2,1)S(1)} %get-tuple-element.18), channel_id=1, source_target_pairs={{0,8},{8,0},{2,10},{10,2},{4,12},{12,4},{6,14},{14,6},{16,24},{24,... | collective-permute-start | bytes 393224 | tf_op jit(solution)/shard_map/ppermute | solution.py:14
  53.9 34.6 %copy-start = (bf16[2,1952,256]{2,1,0:T(8,128)(2,1)S(1)}, bf16[2,1952,256]{2,1,0:T(8,128)(2,1)}, u32[]{:S(2)}) copy-start(bf16[2,1952,256]{2,1,0:T(8,128)(2,1)} %param.7) | copy-start | bytes 5996548
  53.9 5.0 %collective-permute-start.6 = (bf16[2,64,512]{2,1,0:T(8,128)(2,1)S(1)}, bf16[2,64,512]{2,1,0:T(8,128)(2,1)S(1)}, u32[]{:S(2)}, u32[]{:S(2)}) collective-permute-start(bf16[2,64,512]{2,1,0:T(8,128)(2,1)S(1)} %get-tuple-element.33), channel_id=1, source_target_pairs={{0,2},{2,0},{4,6},{6,4},{8,10},{10,8},{12,14},{14,12},{16,18},{18,... | collective-permute-start | bytes 393224 | tf_op jit(solution)/shard_map/ppermute | solution.py:14
  59.0 5.0 %collective-permute-start.7 = (bf16[2,64,512]{2,1,0:T(8,128)(2,1)S(1)}, bf16[2,64,512]{2,1,0:T(8,128)(2,1)S(1)}, u32[]{:S(2)}, u32[]{:S(2)}) collective-permute-start(bf16[2,64,512]{2,1,0:T(8,128)(2,1)S(1)} %fusion.6), channel_id=1, source_target_pairs={{0,4},{4,0},{2,6},{6,2},{8,12},{12,8},{10,14},{14,10},{16,20},{20,... | collective-permute-start | bytes 393224 | tf_op jit(solution)/shard_map/ppermute | solution.py:14
  64.1 5.5 %collective-permute-start.8 = (bf16[2,64,512]{2,1,0:T(8,128)(2,1)S(1)}, bf16[2,64,512]{2,1,0:T(8,128)(2,1)S(1)}, u32[]{:S(2)}, u32[]{:S(2)}) collective-permute-start(bf16[2,64,512]{2,1,0:T(8,128)(2,1)S(1)} %fusion.17), channel_id=1, source_target_pairs={{0,8},{8,0},{2,10},{10,2},{4,12},{12,4},{6,14},{14,6},{16,24},{24,... | collective-permute-start | bytes 393224 | tf_op jit(solution)/shard_map/ppermute | solution.py:14
  69.6 5.9 %collective-permute-start.9 = (bf16[2,64,512]{2,1,0:T(8,128)(2,1)S(1)}, bf16[2,64,512]{2,1,0:T(8,128)(2,1)S(1)}, u32[]{:S(2)}, u32[]{:S(2)}) collective-permute-start(bf16[2,64,512]{2,1,0:T(8,128)(2,1)S(1)} %get-tuple-element.16), channel_id=1, source_target_pairs={{0,16},{16,0},{2,18},{18,2},{4,20},{20,4},{6,22},{22,6},{8,24},{24... | collective-permute-start | bytes 393224 | tf_op jit(solution)/shard_map/ppermute | solution.py:14
  75.8 5.0 %collective-permute-start.10 = (bf16[2,64,512]{2,1,0:T(8,128)(2,1)S(1)}, bf16[2,64,512]{2,1,0:T(8,128)(2,1)S(1)}, u32[]{:S(2)}, u32[]{:S(2)}) collective-permute-start(bf16[2,64,512]{2,1,0:T(8,128)(2,1)S(1)} %get-tuple-element.35), channel_id=1, source_target_pairs={{0,2},{2,0},{4,6},{6,4},{8,10},{10,8},{12,14},{14,12},{16,18},{18,... | collective-permute-start | bytes 393224 | tf_op jit(solution)/shard_map/ppermute | solution.py:14
  80.9 5.0 %collective-permute-start.11 = (bf16[2,64,512]{2,1,0:T(8,128)(2,1)S(1)}, bf16[2,64,512]{2,1,0:T(8,128)(2,1)S(1)}, u32[]{:S(2)}, u32[]{:S(2)}) collective-permute-start(bf16[2,64,512]{2,1,0:T(8,128)(2,1)S(1)} %fusion.7), channel_id=1, source_target_pairs={{0,4},{4,0},{2,6},{6,2},{8,12},{12,8},{10,14},{14,10},{16,20},{20,... | collective-permute-start | bytes 393224 | tf_op jit(solution)/shard_map/ppermute | solution.py:14
  86.0 6.9 %collective-permute-start.12 = (bf16[2,64,512]{2,1,0:T(8,128)(2,1)S(1)}, bf16[2,64,512]{2,1,0:T(8,128)(2,1)S(1)}, u32[]{:S(2)}, u32[]{:S(2)}) collective-permute-start(bf16[2,64,512]{2,1,0:T(8,128)(2,1)S(1)} %fusion.18), channel_id=1, source_target_pairs={{0,8},{8,0},{2,10},{10,2},{4,12},{12,4},{6,14},{14,6},{16,24},{24,... | collective-permute-start | bytes 393224 | tf_op jit(solution)/shard_map/ppermute | solution.py:14
  89.4 43.5 %all-gather.8.cloned.1.call-start = ((), (), s32[]{:S(2)}) async-start(), calls=%async_computation.2 | async-start | bytes 3145728 | tf_op jit(solution)/shard_map/all_gather | solution.py:70
  92.9 7.3 %collective-permute-start.13 = (bf16[2,64,512]{2,1,0:T(8,128)(2,1)S(1)}, bf16[2,64,512]{2,1,0:T(8,128)(2,1)S(1)}, u32[]{:S(2)}, u32[]{:S(2)}) collective-permute-start(bf16[2,64,512]{2,1,0:T(8,128)(2,1)S(1)} %get-tuple-element.14), channel_id=1, source_target_pairs={{0,16},{16,0},{2,18},{18,2},{4,20},{20,4},{6,22},{22,6},{8,24},{24... | collective-permute-start | bytes 393224 | tf_op jit(solution)/shard_map/ppermute | solution.py:14
  100.6 5.0 %collective-permute-start.14 = (bf16[2,64,512]{2,1,0:T(8,128)(2,1)S(1)}, bf16[2,64,512]{2,1,0:T(8,128)(2,1)S(1)}, u32[]{:S(2)}, u32[]{:S(2)}) collective-permute-start(bf16[2,64,512]{2,1,0:T(8,128)(2,1)S(1)} %get-tuple-element.37), channel_id=1, source_target_pairs={{0,2},{2,0},{4,6},{6,4},{8,10},{10,8},{12,14},{14,12},{16,18},{18,... | collective-permute-start | bytes 393224 | tf_op jit(solution)/shard_map/ppermute | solution.py:14
  105.7 5.0 %collective-permute-start.15 = (bf16[2,64,512]{2,1,0:T(8,128)(2,1)S(1)}, bf16[2,64,512]{2,1,0:T(8,128)(2,1)S(1)}, u32[]{:S(2)}, u32[]{:S(2)}) collective-permute-start(bf16[2,64,512]{2,1,0:T(8,128)(2,1)S(1)} %fusion.8), channel_id=1, source_target_pairs={{0,4},{4,0},{2,6},{6,2},{8,12},{12,8},{10,14},{14,10},{16,20},{20,... | collective-permute-start | bytes 393224 | tf_op jit(solution)/shard_map/ppermute | solution.py:14
  110.8 5.0 %collective-permute-start.16 = (bf16[2,64,512]{2,1,0:T(8,128)(2,1)S(1)}, bf16[2,64,512]{2,1,0:T(8,128)(2,1)S(1)}, u32[]{:S(2)}, u32[]{:S(2)}) collective-permute-start(bf16[2,64,512]{2,1,0:T(8,128)(2,1)S(1)} %get-tuple-element.12), channel_id=1, source_target_pairs={{0,8},{8,0},{2,10},{10,2},{4,12},{12,4},{6,14},{14,6},{16,24},{24,... | collective-permute-start | bytes 393224 | tf_op jit(solution)/shard_map/ppermute | solution.py:14
  116.0 5.0 %collective-permute-start.17 = (bf16[2,64,512]{2,1,0:T(8,128)(2,1)S(1)}, bf16[2,64,512]{2,1,0:T(8,128)(2,1)S(1)}, u32[]{:S(2)}, u32[]{:S(2)}) collective-permute-start(bf16[2,64,512]{2,1,0:T(8,128)(2,1)S(1)} %get-tuple-element.39), channel_id=1, source_target_pairs={{0,2},{2,0},{4,6},{6,4},{8,10},{10,8},{12,14},{14,12},{16,18},{18,... | collective-permute-start | bytes 393224 | tf_op jit(solution)/shard_map/ppermute | solution.py:14
  121.1 5.0 %collective-permute-start.18 = (bf16[2,64,512]{2,1,0:T(8,128)(2,1)S(1)}, bf16[2,64,512]{2,1,0:T(8,128)(2,1)S(1)}, u32[]{:S(2)}, u32[]{:S(2)}) collective-permute-start(bf16[2,64,512]{2,1,0:T(8,128)(2,1)S(1)} %get-tuple-element.10), channel_id=1, source_target_pairs={{0,4},{4,0},{2,6},{6,2},{8,12},{12,8},{10,14},{14,10},{16,20},{20,... | collective-permute-start | bytes 393224 | tf_op jit(solution)/shard_map/ppermute | solution.py:14
  127.7 5.0 %collective-permute-start.19 = (bf16[2,64,512]{2,1,0:T(8,128)(2,1)S(1)}, bf16[2,64,512]{2,1,0:T(8,128)(2,1)S(1)}, u32[]{:S(2)}, u32[]{:S(2)}) collective-permute-start(bf16[2,64,512]{2,1,0:T(8,128)(2,1)S(1)} %get-tuple-element.41), channel_id=1, source_target_pairs={{0,2},{2,0},{4,6},{6,4},{8,10},{10,8},{12,14},{14,12},{16,18},{18,... | collective-permute-start | bytes 393224 | tf_op jit(solution)/shard_map/ppermute | solution.py:14
  (8 other events, 121.5 us)
Sparse Core Ops, SparseCore 0:
  8.9 11.6 all-gather.3
  89.5 9.3 all-gather.5
  108.4 9.9 all-gather.7
where the time goes:
time: 142 us
  waiting for transfers between devices  69.5 us (49%)
  starting transfers between devices  34.9 us (25%)
  between operations  13.4 us (9%)
  blocking collectives  12 us (8%)
  matrix products  6.97 us (5%)
  local copies, waits for them, and re-layouts  4.35 us (3%)
    ppermute x20, waiting for transfers between devices, partner(): return lax.ppermute(block, axis, route)  57.7 us
    ppermute x20, starting transfers between devices, partner(): return lax.ppermute(block, axis, route)  34.9 us
    all_gather x6, blocking collectives, per_device(): lax.all_gather(factor_rows, 'rhs', axis=2, tiled=True)  12 us
    all_gather x3, waiting for transfers between devices, per_device(): lax.all_gather(factor_rows, 'rhs', axis=2, tiled=True)  11.7 us
    dot_general x9, matrix products, project_with(): jnp.einsum('bcr,brm->bcm', block, piece, preferred_element_type=jnp.float32)  6.97 us
  transfers between devices with their start and end apart: 23, of which 21 were waited for; matrix products, arithmetic and copies ran while one was open for 3% of the time, Pallas kernels for 0%

commit v1 on v0

v1 whole, which is shorter than its diff:
```python
import functools

import jax
import jax.numpy as jnp
from jax import lax
from jax.experimental import pallas as pl
from jax.experimental.pallas import tpu as pltpu
from jax.sharding import PartitionSpec as P

MESH = pl.DeviceIdType.MESH
UNROLL = 16


def folds_of(width):
    return 1 if width >= 128 else min(128 // width, 4)


def make_phases(levels, width_all):
    phases = []
    for level in range(levels):
        group = 2 << level
        phases.append((group, group, width_all // group))
    for level in range(levels, 0, -1):
        group = 1 << level
        phases.append((group, group // 2, width_all // (group // 2)))
    return phases


def make_chunks(levels, width_all, up_rows, down_rows):
    ups = [(2 * width_all - (2 * width_all >> l), width_all >> l) for l in range(levels)]
    root = width_all >> levels
    downs = [
        (root + 2 * (2 * width_all - (2 * width_all >> l)), 2 * (width_all >> l))
        for l in range(levels)
    ]
    fine = all(o % 16 == 0 and w % 16 == 0 for o, w in ups + downs + [(0, root)])
    if not fine:
        chunks = [(False, None, 0, up_rows), (True, None, 0, down_rows)]
        return chunks, [[0]] * levels, [1], [[1]] * levels
    chunks = [(False, 0) + ups[0], (False, 1) + ups[0]]
    up_at = [[0, 1]]
    for l in range(1, levels):
        up_at.append([len(chunks)])
        chunks.append((False, None) + ups[l])
    root_at = [len(chunks)]
    chunks.append((True, None, 0, root))
    down_at = [None] * levels
    for l in reversed(range(levels)):
        down_at[l] = [len(chunks)]
        chunks.append((True, None) + downs[l])
    return chunks, up_at, root_at, down_at


def kernel(dims, skel_hbm, ranks, up_hbm, down_hbm, out, *scratch):
    levels, width_all, boxes, rhs, n_leaf, up_rows, down_rows = dims
    phases = make_phases(levels, width_all)
    chunks, up_at, root_at, down_at = make_chunks(levels, width_all, up_rows, down_rows)
    count = len(phases)
    skel, up, down, own_sum = scratch[:4]
    sends = scratch[4 : 4 + count]
    recvs = scratch[4 + count : 4 + 2 * count]
    skel_sem, local_sem, w_send, w_recv, p_send, p_recv = scratch[4 + 2 * count :]

    leaf = lax.axis_index("leaf")
    core = lax.axis_index("rhs")
    other = 1 - core
    span = 1 << levels
    span_base = leaf - leaf % span

    barrier = pltpu.get_barrier_semaphore()
    pl.semaphore_signal(barrier, inc=1, device_id=(leaf, other), device_id_type=MESH)

    def greet(d):
        target = span_base + (leaf + d) % span
        pl.semaphore_signal(barrier, inc=1, device_id=(target, core), device_id_type=MESH)

    if span <= UNROLL:
        for d in range(1, span):
            greet(d)
    else:
        pl.loop(1, span)(greet)

    def box_rows(chunk):
        is_down, box, first, rows = chunk
        boxes_of = slice(None) if box is None else pl.ds(box, 1)
        source = (down_hbm if is_down else up_hbm).at[boxes_of, pl.ds(first, rows), :]
        target = (down if is_down else up).at[core, boxes_of, pl.ds(first, rows), :]
        return source, target

    def arriving(chunk):
        is_down, box, first, rows = chunk
        boxes_of = slice(None) if box is None else pl.ds(box, 1)
        return (down if is_down else up).at[other, boxes_of, pl.ds(first, rows), :]

    skel_copy = pltpu.make_async_copy(skel_hbm, skel, skel_sem)
    skel_copy.start()
    local = []
    for i, chunk in enumerate(chunks):
        source, target = box_rows(chunk)
        copy = pltpu.make_async_copy(source, target, local_sem.at[i])
        copy.start()
        local.append(copy)

    pl.semaphore_wait(barrier, span)

    remote = []
    for i, chunk in enumerate(chunks):
        source, target = box_rows(chunk)
        copy = pltpu.make_async_remote_copy(
            src_ref=source,
            dst_ref=target,
            send_sem=w_send.at[i],
            recv_sem=w_recv.at[i],
            device_id=(leaf, other),
            device_id_type=MESH,
        )
        copy.start()
        remote.append(copy)

    ready = set()

    def need(indices, box):
        for i in indices:
            if i in ready or chunks[i][1] not in (None, box):
                continue
            ready.add(i)
            local[i].wait()
            landed = arriving(chunks[i])
            pltpu.make_async_copy(landed, landed, w_recv.at[i]).wait()

    def times(block, weights, box, first, rows):
        return jnp.concatenate(
            [
                jnp.dot(
                    block,
                    weights[half, box, first : first + rows, :],
                    preferred_element_type=jnp.float32,
                )
                for half in range(2)
            ],
            axis=1,
        )

    def send(phase, box, value):
        group, slices, width = phases[phase]
        member = leaf % group
        base = leaf - member
        folds = folds_of(width)
        rows = rhs // folds
        value = value.astype(jnp.bfloat16)
        for k in range(slices):
            piece = value[:, k * width : (k + 1) * width]
            if folds > 1:
                piece = jnp.concatenate(
                    [piece[f * rows : (f + 1) * rows] for f in range(folds)], axis=1
                )
            sends[phase][box, k] = piece

        def one(d):
            there = (member + d) % group
            pltpu.make_async_remote_copy(
                src_ref=sends[phase].at[box, there % slices],
                dst_ref=recvs[phase].at[box, d - 1],
                send_sem=p_send.at[phase, box],
                recv_sem=p_recv.at[phase, box],
                device_id=(base + there, core),
                device_id_type=MESH,
            ).start()

        if group <= UNROLL:
            for d in range(1, group):
                one(d)
        else:
            pl.loop(1, group)(one)

    def keep(value, rank, first_column, width):
        columns = lax.broadcasted_iota(jnp.int32, value.shape, 1) % width + first_column
        return jnp.where(columns % (width_all // 2) < rank, value, 0.0)

    def receive(phase, box, level):
        group, slices, width = phases[phase]
        mine = leaf % slices
        folds = folds_of(width)
        rows = rhs // folds
        landed = recvs[phase].at[box]
        pltpu.make_async_copy(landed, landed, p_recv.at[phase, box]).wait()
        total = sends[phase][box, mine].astype(jnp.float32)
        if group <= UNROLL:
            for d in range(group - 1):
                total = total + recvs[phase][box, d].astype(jnp.float32)
        else:
            total = total + jnp.sum(recvs[phase][box].astype(jnp.float32), axis=0)
        total = keep(total, ranks[box, 0, level], mine * width, width)
        if folds > 1:
            total = jnp.concatenate(
                [total[:, f * width : (f + 1) * width] for f in range(folds)], axis=0
            )
        return total.astype(jnp.bfloat16)

    def down_first(level):
        return (width_all >> levels) + 2 * (2 * width_all - (2 * width_all >> level))

    saved = [[None] * boxes for _ in range(levels + 1)]

    def own_terms(level):
        width = width_all >> level
        for box in range(boxes):
            need(down_at[level], box)
            own_sum[level, box] = times(saved[level][box], down, box, down_first(level), width)

    skel_copy.wait()
    for level in range(levels):
        width = width_all >> level
        offset = 2 * width_all - (2 * width_all >> level)
        for box in range(boxes):
            if level == 0:
                block = keep(
                    skel[box, 0].astype(jnp.float32), ranks[box, 0, 0], 0, width_all
                ).astype(jnp.bfloat16)
            else:
                block = receive(level - 1, box, level)
            saved[level][box] = block
            need(up_at[level], box)
            send(level, box, times(block, up, box, offset, width))
        if level == levels - 1:
            own_terms(level)
            if level - 1 > 1:
                own_terms(level - 1)
    phase = levels
    for box in range(boxes):
        block = receive(levels - 1, box, levels)
        need(root_at, box)
        send(phase, box, times(block, down, box, 0, width_all >> levels))
    for level in reversed(range(levels - 2 if levels - 2 > 1 else levels - 1)):
        own_terms(level)
    for level in reversed(range(levels)):
        width = width_all >> level
        for box in range(boxes):
            block = receive(phase, box, level + 1)
            value = own_sum[level, box] + times(
                block, down, box, down_first(level) + width, width
            )
            if level:
                send(phase + 1, box, value)
            else:
                out[box, 0] = keep(value, ranks[box, 0, 0], 0, width_all).astype(out.dtype)
        phase += 1

    for copy in remote:
        copy.wait_send()
    for p, (group, slices, width) in enumerate(phases):
        for box in range(boxes):
            sent = recvs[p].at[box]
            pltpu.make_async_copy(sent, sent, p_send.at[p, box]).wait()


def per_device(dims, leaf_skel, ranks, up_weight, down_weight):
    levels, width_all, boxes, rhs, n_leaf, up_rows, down_rows = dims
    phases = make_phases(levels, width_all)
    chunks = make_chunks(levels, width_all, up_rows, down_rows)[0]
    half = up_weight.shape[-1]

    def piece(width):
        folds = folds_of(width)
        return rhs // folds, folds * width

    sends = [pltpu.VMEM((boxes, s) + piece(w), jnp.bfloat16) for g, s, w in phases]
    recvs = [pltpu.VMEM((boxes, g - 1) + piece(w), jnp.bfloat16) for g, s, w in phases]
    dma = pltpu.SemaphoreType.DMA
    return pl.pallas_call(
        functools.partial(kernel, dims),
        out_shape=jax.ShapeDtypeStruct(leaf_skel.shape, leaf_skel.dtype),
        in_specs=[
            pl.BlockSpec(memory_space=pl.ANY),
            pl.BlockSpec(memory_space=pltpu.SMEM),
            pl.BlockSpec(memory_space=pl.ANY),
            pl.BlockSpec(memory_space=pl.ANY),
        ],
        out_specs=pl.BlockSpec(memory_space=pltpu.VMEM),
        scratch_shapes=[
            pltpu.VMEM(leaf_skel.shape, jnp.bfloat16),
            pltpu.VMEM((2, boxes, up_rows, half), jnp.bfloat16),
            pltpu.VMEM((2, boxes, down_rows, half), jnp.bfloat16),
            pltpu.VMEM((levels, boxes, rhs, width_all), jnp.float32),
        ]
        + sends
        + recvs
        + [
            dma,
            dma((len(chunks),)),
            dma((len(chunks),)),
            dma((len(chunks),)),
            dma((len(phases), boxes)),
            dma((len(phases), boxes)),
        ],
        compiler_params=pltpu.CompilerParams(
            collective_id=0, has_side_effects=True, vmem_limit_bytes=48 * 1024 * 1024
        ),
        cost_estimate=pl.CostEstimate(
            flops=4 * boxes * rhs * (up_rows + down_rows) * half * 2,
            bytes_accessed=4 * boxes * (up_rows + down_rows) * half,
            transcendentals=0,
        ),
    )(leaf_skel, ranks, up_weight, down_weight)


def solution(mesh):
    n_leaf, n_rhs = mesh.shape["leaf"], mesh.shape["rhs"]

    def whole(leaf_skel, ranks, up_weight, down_weight):
        dims = (
            ranks.shape[-1] - 1,
            leaf_skel.shape[-1],
            leaf_skel.shape[0],
            leaf_skel.shape[2] // n_rhs,
            n_leaf,
            up_weight.shape[1] // n_leaf,
            down_weight.shape[1] // n_leaf,
        )
        return jax.shard_map(
            functools.partial(per_device, dims),
            mesh=mesh,
            in_specs=(
                P(None, "leaf", "rhs", None),
                P(None, "leaf", None),
                P(None, "leaf", "rhs"),
                P(None, "leaf", "rhs"),
            ),
            out_specs=P(None, "leaf", "rhs", None),
            check_vma=False,
        )(leaf_skel, ranks, up_weight, down_weight)

    return whole
```

time: 142 us -> 48.2 us (0.34)
  waiting for transfers between devices: 69.5 us -> 0 us
  Pallas kernels: 0 us -> 43 us
  starting transfers between devices: 34.9 us -> 0 us
  between operations: 13.4 us -> 0.01 us
  blocking collectives: 12 us -> 0 us
  matrix products: 6.97 us -> 0 us
    ppermute x20 -> x0, waiting for transfers between devices: 57.7 us -> none  [partner(): return lax.ppermute(block, axis, route)]
    pallas_call x0 -> x1, Pallas kernels: none -> 43 us  [per_device(): pl.pallas_call(functools.partial(kernel, dims), out_shape=jax.ShapeDtypeS...]
    ppermute x20 -> x0, starting transfers between devices: 34.9 us -> none  [partner(): return lax.ppermute(block, axis, route)]
    all_gather x6 -> x0, blocking collectives: 12 us -> none  [per_device(): lax.all_gather(factor_rows, 'rhs', axis=2, tiled=True)]
    all_gather x3 -> x0, waiting for transfers between devices: 11.7 us -> none  [per_device(): lax.all_gather(factor_rows, 'rhs', axis=2, tiled=True)]
    dot_general x9 -> x0, matrix products: 6.97 us -> none  [project_with(): jnp.einsum('bcr,brm->bcm', block, piece, preferred_element_type=jnp.float32)]
    unnamed x6 -> x9, local copies, waits for them, and re-layouts: 0.01 us -> 5 us
    slice x16 -> x0, local copies, waits for them, and re-layouts: 4.09 us -> none  [the longest x7 1.95 us: per_device(): factor_rows = up_weight[:, offset:offset + width, :]]
  transfers between devices with their start and end apart: 23 -> 0, of which waited for: 21 -> 0; matrix products, arithmetic and copies ran while one was open for 3% -> 0% of each run, Pallas kernels for 0% -> 0%
where the time goes in v1:
time: 48.2 us; the launch traced here: 48 us
  Pallas kernels  43 us (89%)
  local copies, waits for them, and re-layouts  5 us (10%)
    pallas_call x1, Pallas kernels, per_device(): pl.pallas_call(functools.partial(kernel, dims), out_shape=jax.ShapeDtypeS...  43 us
    unnamed x9, local copies, waits for them, and re-layouts  5 us

profile of v1, /device:TPU:0, one launch (start us, length us, event | category | flops | bytes accessed | tf_op | source)
XLA Modules:
  0.0 48.0 jit_solution(4214709367149939063)
XLA Ops:
  0.0 0.0 copy-start
  0.0 1.6 %copy-done = bf16[2,1952,256]{2,1,0:T(8,128)(2,1)S(1)} copy-done((bf16[2,1952,256]{2,1,0:T(8,128)(2,1)S(1)}, bf16[2,1952,256]{2,1,0:T(8,128)(2,1)}, u32[]{:S(2)}) %copy-start) | copy-done | bytes 1998872
  1.6 0.0 copy-start.1
  1.6 1.2 %copy-done.1 = bf16[2,960,256]{2,1,0:T(8,128)(2,1)S(1)} copy-done((bf16[2,960,256]{2,1,0:T(8,128)(2,1)S(1)}, bf16[2,960,256]{2,1,0:T(8,128)(2,1)}, u32[]{:S(2)}) %copy-start.1) | copy-done | bytes 983064
  2.8 0.0 copy-start.2
  2.8 0.9 %copy-done.2 = bf16[2,1,64,512]{3,2,1,0:T(8,128)(2,1)S(1)} copy-done((bf16[2,1,64,512]{3,2,1,0:T(8,128)(2,1)S(1)}, bf16[2,1,64,512]{3,2,1,0:T(8,128)(2,1)}, u32[]{:S(2)}) %copy-start.2) | copy-done | bytes 131096
  3.7 0.0 copy-start.3
  3.7 0.7 %copy-done.3 = s32[2,1,5]{2,1,0:T(1,128)S(1)} copy-done((s32[2,1,5]{2,1,0:T(1,128)S(1)}, s32[2,1,5]{2,1,0:T(1,128)}, u32[]{:S(2)}) %copy-start.3) | copy-done | bytes 64
  4.3 43.0 %shard_map.46 = bf16[2,1,64,512]{3,2,1,0:T(8,128)(2,1)S(1)} custom-call(bf16[2,1,64,512]{3,2,1,0:T(8,128)(2,1)S(1)} %copy-done.2, s32[2,1,5]{2,1,0:T(1,128)S(1)} %copy-done.3, bf16[2,960,256]{2,1,0:T(8,128)(2,1)S(1)} %copy-done.1, bf16[2,1952,256]{2,1,0:T(8,128)(2,1)S(1)} %copy-done), custom_call_target="tpu_custom_call" | custom-call | flops 763363328 | bytes 5963776 | tf_op jit(solution)/shard_map/pallas_call | solution.py:270
  47.4 0.7 %copy.6 = bf16[2,1,64,512]{3,2,1,0:T(8,128)(2,1)} copy(bf16[2,1,64,512]{3,2,1,0:T(8,128)(2,1)S(1)} %shard_map.46) | data formatting | bytes 262144
Async XLA Ops:
  0.0 1.6 %copy-start = (bf16[2,1952,256]{2,1,0:T(8,128)(2,1)S(1)}, bf16[2,1952,256]{2,1,0:T(8,128)(2,1)}, u32[]{:S(2)}) copy-start(bf16[2,1952,256]{2,1,0:T(8,128)(2,1)} %down_hbm.1) | copy-start | bytes 5996548
  1.6 1.2 %copy-start.1 = (bf16[2,960,256]{2,1,0:T(8,128)(2,1)S(1)}, bf16[2,960,256]{2,1,0:T(8,128)(2,1)}, u32[]{:S(2)}) copy-start(bf16[2,960,256]{2,1,0:T(8,128)(2,1)} %up_hbm.1) | copy-start | bytes 2949124
  2.8 0.9 %copy-start.2 = (bf16[2,1,64,512]{3,2,1,0:T(8,128)(2,1)S(1)}, bf16[2,1,64,512]{3,2,1,0:T(8,128)(2,1)}, u32[]{:S(2)}) copy-start(bf16[2,1,64,512]{3,2,1,0:T(8,128)(2,1)} %skel_hbm.1) | copy-start | bytes 393220
  3.7 0.7 %copy-start.3 = (s32[2,1,5]{2,1,0:T(1,128)S(1)}, s32[2,1,5]{2,1,0:T(1,128)}, u32[]{:S(2)}) copy-start(s32[2,1,5]{2,1,0:T(1,128)} %ranks.1) | copy-start | bytes 124

commit v2 on v1

--- a/solution.py
+++ b/solution.py
@@ -13,6 +13,12 @@
 
 def folds_of(width):
     return 1 if width >= 128 else min(128 // width, 4)
+
+
+def far_first(group):
+    hops = [1, 1, 1, 2]
+    count = lambda d: sum(h for bit, h in enumerate(hops) if d >> bit & 1)
+    return sorted(range(1, group), key=count, reverse=True)
 
 
 def make_phases(levels, width_all):
@@ -51,34 +57,27 @@
     return chunks, up_at, root_at, down_at
 
 
-def kernel(dims, skel_hbm, ranks, up_hbm, down_hbm, out, *scratch):
+def kernel(dims, skel_hbm, ranks_hbm, up_hbm, down_hbm, out, *scratch):
     levels, width_all, boxes, rhs, n_leaf, up_rows, down_rows = dims
     phases = make_phases(levels, width_all)
     chunks, up_at, root_at, down_at = make_chunks(levels, width_all, up_rows, down_rows)
     count = len(phases)
-    skel, up, down, own_sum = scratch[:4]
-    sends = scratch[4 : 4 + count]
-    recvs = scratch[4 + count : 4 + 2 * count]
-    skel_sem, local_sem, w_send, w_recv, p_send, p_recv = scratch[4 + 2 * count :]
+    skel, ranks, up, down, own_sum = scratch[:5]
+    sends = scratch[5 : 5 + count]
+    recvs = scratch[5 + count : 5 + 2 * count]
+    skel_sem, ranks_sem, local_sem, w_send, w_recv, p_send, p_recv = scratch[5 + 2 * count :]
 
     leaf = lax.axis_index("leaf")
     core = lax.axis_index("rhs")
     other = 1 - core
-    span = 1 << levels
-    span_base = leaf - leaf % span
 
     barrier = pltpu.get_barrier_semaphore()
     pl.semaphore_signal(barrier, inc=1, device_id=(leaf, other), device_id_type=MESH)
 
-    def greet(d):
-        target = span_base + (leaf + d) % span
+    for bit in range(levels):
+        step = 1 << bit
+        target = leaf + step * (1 - 2 * (leaf // step % 2))
         pl.semaphore_signal(barrier, inc=1, device_id=(target, core), device_id_type=MESH)
-
-    if span <= UNROLL:
-        for d in range(1, span):
-            greet(d)
-    else:
-        pl.loop(1, span)(greet)
 
     def box_rows(chunk):
         is_down, box, first, rows = chunk
@@ -94,6 +93,8 @@
 
     skel_copy = pltpu.make_async_copy(skel_hbm, skel, skel_sem)
     skel_copy.start()
+    ranks_copy = pltpu.make_async_copy(ranks_hbm, ranks, ranks_sem)
+    ranks_copy.start()
     local = []
     for i, chunk in enumerate(chunks):
         source, target = box_rows(chunk)
@@ -101,7 +102,7 @@
         copy.start()
         local.append(copy)
 
-    pl.semaphore_wait(barrier, span)
+    pl.semaphore_wait(barrier, levels + 1)
 
     remote = []
     for i, chunk in enumerate(chunks):
@@ -157,7 +158,10 @@
             sends[phase][box, k] = piece
 
         def one(d):
-            there = (member + d) % group
+            there = member
+            for bit in range(group.bit_length() - 1):
+                step = 1 << bit
+                there = there + step * (d // step % 2) * (1 - 2 * (member // step % 2))
             pltpu.make_async_remote_copy(
                 src_ref=sends[phase].at[box, there % slices],
                 dst_ref=recvs[phase].at[box, d - 1],
@@ -168,7 +172,7 @@
             ).start()
 
         if group <= UNROLL:
-            for d in range(1, group):
+            for d in far_first(group):
                 one(d)
         else:
             pl.loop(1, group)(one)
@@ -209,6 +213,7 @@
             own_sum[level, box] = times(saved[level][box], down, box, down_first(level), width)
 
     skel_copy.wait()
+    ranks_copy.wait()
     for level in range(levels):
         width = width_all >> level
         offset = 2 * width_all - (2 * width_all >> level)
@@ -270,15 +275,11 @@
     return pl.pallas_call(
         functools.partial(kernel, dims),
         out_shape=jax.ShapeDtypeStruct(leaf_skel.shape, leaf_skel.dtype),
-        in_specs=[
-            pl.BlockSpec(memory_space=pl.ANY),
-            pl.BlockSpec(memory_space=pltpu.SMEM),
-            pl.BlockSpec(memory_space=pl.ANY),
-            pl.BlockSpec(memory_space=pl.ANY),
-        ],
+        in_specs=[pl.BlockSpec(memory_space=pltpu.HBM)] * 4,
         out_specs=pl.BlockSpec(memory_space=pltpu.VMEM),
         scratch_shapes=[
             pltpu.VMEM(leaf_skel.shape, jnp.bfloat16),
+            pltpu.SMEM(ranks.shape, jnp.int32),
             pltpu.VMEM((2, boxes, up_rows, half), jnp.bfloat16),
             pltpu.VMEM((2, boxes, down_rows, half), jnp.bfloat16),
             pltpu.VMEM((levels, boxes, rhs, width_all), jnp.float32),
@@ -287,6 +288,7 @@
         + recvs
         + [
             dma,
+            dma,
             dma((len(chunks),)),
             dma((len(chunks),)),
             dma((len(chunks),)),
@@ -294,7 +296,7 @@
             dma((len(phases), boxes)),
         ],
         compiler_params=pltpu.CompilerParams(
-            collective_id=0, has_side_effects=True, vmem_limit_bytes=48 * 1024 * 1024
+            collective_id=0, has_side_effects=True, vmem_limit_bytes=60 * 1024 * 1024
         ),
         cost_estimate=pl.CostEstimate(
             flops=4 * boxes * rhs * (up_rows + down_rows) * half * 2,

time: 48.2 us -> 42.2 us (0.88)
  local copies, waits for them, and re-layouts: 5 us -> 1.57 us
  Pallas kernels: 43 us -> 40.5 us
    unnamed x9 -> x1, local copies, waits for them, and re-layouts: 5 us -> 1.57 us
    pallas_call x1, Pallas kernels: 43 us -> 40.5 us  [per_device(): pl.pallas_call(functools.partial(kernel, dims), out_shape=jax.ShapeDtypeS...]
where the time goes in v2:
time: 42.2 us; the launch traced here: 42 us
  Pallas kernels  40.5 us (96%)
  local copies, waits for them, and re-layouts  1.57 us (4%)
    pallas_call x1, Pallas kernels, per_device(): pl.pallas_call(functools.partial(kernel, dims), out_shape=jax.ShapeDtypeS...  40.5 us
    unnamed x1, local copies, waits for them, and re-layouts  1.57 us

profile of v2, /device:TPU:0, one launch (start us, length us, event | category | flops | bytes accessed | tf_op | source)
XLA Modules:
  0.0 42.0 jit_solution(452313045233225668)
XLA Ops:
  0.0 40.5 %shard_map.46 = bf16[2,1,64,512]{3,2,1,0:T(8,128)(2,1)} custom-call(bf16[2,1,64,512]{3,2,1,0:T(8,128)(2,1)} %skel_hbm.1, s32[2,1,5]{2,1,0:T(1,128)} %ranks_hbm.1, bf16[2,960,256]{2,1,0:T(8,128)(2,1)} %up_hbm.1, bf16[2,1952,256]{2,1,0:T(8,128)(2,1)} %down_hbm.1), custom_call_target="tpu_custom_call" | custom-call | flops 763363328 | bytes 5963776 | tf_op jit(solution)/shard_map/pallas_call | solution.py:275
  40.5 1.6 %copy.6 = bf16[2,1,64,512]{3,2,1,0:T(8,128)(2,1)} copy(bf16[2,1,64,512]{3,2,1,0:T(8,128)(2,1)} %shard_map.46) | data formatting | bytes 262144

commit v3 on v2

--- a/solution.py
+++ b/solution.py
@@ -28,7 +28,8 @@
         phases.append((group, group, width_all // group))
     for level in range(levels, 0, -1):
         group = 1 << level
-        phases.append((group, group // 2, width_all // (group // 2)))
+        slices = 1 if level == 2 else group // 2
+        phases.append((group, slices, width_all // slices))
     return phases
 
 
@@ -62,10 +63,11 @@
     phases = make_phases(levels, width_all)
     chunks, up_at, root_at, down_at = make_chunks(levels, width_all, up_rows, down_rows)
     count = len(phases)
-    skel, ranks, up, down, own_sum = scratch[:5]
-    sends = scratch[5 : 5 + count]
-    recvs = scratch[5 + count : 5 + 2 * count]
-    skel_sem, ranks_sem, local_sem, w_send, w_recv, p_send, p_recv = scratch[5 + 2 * count :]
+    skel, ranks, up, down, own_sum, pair = scratch[:6]
+    sends = scratch[6 : 6 + count]
+    recvs = scratch[6 + count : 6 + 2 * count]
+    skel_sem, ranks_sem, local_sem, w_send, w_recv, p_send, p_recv = scratch[6 + 2 * count : -2]
+    pair_send, pair_recv = scratch[-2:]
 
     leaf = lax.axis_index("leaf")
     core = lax.axis_index("rhs")
@@ -117,6 +119,30 @@
         )
         copy.start()
         remote.append(copy)
+
+    width_pair = width_all // 2
+    pair_rows = (width_all >> levels) + 2 * width_all + width_pair
+    parity = leaf % 2
+    part = width_pair // 2
+    to_pair = [
+        pltpu.make_async_remote_copy(
+            src_ref=down_hbm.at[pl.ds(i // 2, 1), pl.ds(pair_rows + i % 2 * part, part), :],
+            dst_ref=pair.at[core, pl.ds(i // 2, 1), pl.ds(i % 2 * part, part), :],
+            send_sem=pair_send.at[1 + i],
+            recv_sem=pair_recv.at[1 + i],
+            device_id=(leaf + 1 - 2 * parity, core),
+            device_id_type=MESH,
+        )
+        for i in range(2 * boxes)
+    ]
+    to_core = pltpu.make_async_remote_copy(
+        src_ref=pair.at[core],
+        dst_ref=pair.at[core],
+        send_sem=pair_send.at[0],
+        recv_sem=pair_recv.at[0],
+        device_id=(leaf, other),
+        device_id_type=MESH,
+    )
 
     ready = set()
 
@@ -181,11 +207,9 @@
         columns = lax.broadcasted_iota(jnp.int32, value.shape, 1) % width + first_column
         return jnp.where(columns % (width_all // 2) < rank, value, 0.0)
 
-    def receive(phase, box, level):
+    def gather(phase, box):
         group, slices, width = phases[phase]
         mine = leaf % slices
-        folds = folds_of(width)
-        rows = rhs // folds
         landed = recvs[phase].at[box]
         pltpu.make_async_copy(landed, landed, p_recv.at[phase, box]).wait()
         total = sends[phase][box, mine].astype(jnp.float32)
@@ -194,7 +218,13 @@
                 total = total + recvs[phase][box, d].astype(jnp.float32)
         else:
             total = total + jnp.sum(recvs[phase][box].astype(jnp.float32), axis=0)
-        total = keep(total, ranks[box, 0, level], mine * width, width)
+        return total
+
+    def receive(phase, box, level):
+        group, slices, width = phases[phase]
+        mine = leaf % slices
+        folds = folds_of(width)
+        total = keep(gather(phase, box), ranks[box, 0, level], mine * width, width)
         if folds > 1:
             total = jnp.concatenate(
                 [total[:, f * width : (f + 1) * width] for f in range(folds)], axis=0
@@ -210,7 +240,11 @@
         width = width_all >> level
         for box in range(boxes):
             need(down_at[level], box)
-            own_sum[level, box] = times(saved[level][box], down, box, down_first(level), width)
+            terms = times(saved[level][box], down, box, down_first(level), width)
+            if level == 1:
+                send(count - 1, box, terms)
+            else:
+                own_sum[level, box] = terms
 
     skel_copy.wait()
     ranks_copy.wait()
@@ -227,6 +261,8 @@
             saved[level][box] = block
             need(up_at[level], box)
             send(level, box, times(block, up, box, offset, width))
+        for copy in to_pair[level:] if level == levels - 1 else to_pair[level : level + 1]:
+            copy.start()
         if level == levels - 1:
             own_terms(level)
             if level - 1 > 1:
@@ -238,10 +274,29 @@
         send(phase, box, times(block, down, box, 0, width_all >> levels))
     for level in reversed(range(levels - 2 if levels - 2 > 1 else levels - 1)):
         own_terms(level)
+    for copy in to_pair:
+        copy.wait_recv()
+    to_core.start()
     for level in reversed(range(levels)):
         width = width_all >> level
+        if level == 1:
+            phase += 1
+            continue
         for box in range(boxes):
-            block = receive(phase, box, level + 1)
+            if level:
+                block = receive(phase, box, level + 1)
+            else:
+                above = receive(phase - 1, box, 2)
+                if box == 0:
+                    arrived = pair.at[other]
+                    pltpu.make_async_copy(arrived, arrived, pair_recv.at[0]).wait()
+                low, high = above[:, :width_pair], above[:, width_pair:]
+                mine = jnp.where(parity == 0, low, high)
+                theirs = jnp.where(parity == 0, high, low)
+                total = gather(phase, box)
+                total = total + times(mine, down, box, pair_rows, width_pair)
+                total = total + times(theirs, pair, box, 0, width_pair)
+                block = keep(total, ranks[box, 0, 1], 0, width_all).astype(jnp.bfloat16)
             value = own_sum[level, box] + times(
                 block, down, box, down_first(level) + width, width
             )
@@ -251,7 +306,7 @@
                 out[box, 0] = keep(value, ranks[box, 0, 0], 0, width_all).astype(out.dtype)
         phase += 1
 
-    for copy in remote:
+    for copy in remote + to_pair + [to_core]:
         copy.wait_send()
     for p, (group, slices, width) in enumerate(phases):
         for box in range(boxes):
@@ -283,6 +338,7 @@
             pltpu.VMEM((2, boxes, up_rows, half), jnp.bfloat16),
             pltpu.VMEM((2, boxes, down_rows, half), jnp.bfloat16),
             pltpu.VMEM((levels, boxes, rhs, width_all), jnp.float32),
+            pltpu.VMEM((2, boxes, width_all // 2, half), jnp.bfloat16),
         ]
         + sends
         + recvs
@@ -294,6 +350,8 @@
             dma((len(chunks),)),
             dma((len(phases), boxes)),
             dma((len(phases), boxes)),
+            dma((1 + 2 * boxes,)),
+            dma((1 + 2 * boxes,)),
         ],
         compiler_params=pltpu.CompilerParams(
             collective_id=0, has_side_effects=True, vmem_limit_bytes=60 * 1024 * 1024

time: 42.2 us -> 40.1 us (0.950)
  Pallas kernels: 40.5 us -> 38.4 us
    pallas_call x1, Pallas kernels: 40.5 us -> 38.4 us  [per_device(): pl.pallas_call(functools.partial(kernel, dims), out_shape=jax.ShapeDtypeS...]
where the time goes in v3:
time: 40.1 us; the launch traced here: 40 us
  Pallas kernels  38.4 us (96%)
  local copies, waits for them, and re-layouts  1.57 us (4%)
    pallas_call x1, Pallas kernels, per_device(): pl.pallas_call(functools.partial(kernel, dims), out_shape=jax.ShapeDtypeS...  38.4 us
    unnamed x1, local copies, waits for them, and re-layouts  1.57 us

profile of v3, /device:TPU:0, one launch (start us, length us, event | category | flops | bytes accessed | tf_op | source)
XLA Modules:
  0.0 40.0 jit_solution(16840091188822092884)
XLA Ops:
  0.0 38.4 %shard_map.46 = bf16[2,1,64,512]{3,2,1,0:T(8,128)(2,1)} custom-call(bf16[2,1,64,512]{3,2,1,0:T(8,128)(2,1)} %skel_hbm.1, s32[2,1,5]{2,1,0:T(1,128)} %ranks_hbm.1, bf16[2,960,256]{2,1,0:T(8,128)(2,1)} %up_hbm.1, bf16[2,1952,256]{2,1,0:T(8,128)(2,1)} %down_hbm.1), custom_call_target="tpu_custom_call" | custom-call | flops 763363328 | bytes 5963776 | tf_op jit(solution)/shard_map/pallas_call | solution.py:330
  38.4 1.6 %copy.6 = bf16[2,1,64,512]{3,2,1,0:T(8,128)(2,1)} copy(bf16[2,1,64,512]{3,2,1,0:T(8,128)(2,1)} %shard_map.46) | data formatting | bytes 262144
